TPU v7x, 32 devices: a whole 2x2x4 slice. The times are simulated.
32 devices in a mesh: lat: 16 (over z, x, core), ma: 2 (over y).
Axes of the slice: x: 2, y: 2, z: 4, core: 2. Of those that a mesh axis runs over, the one named last changes fastest.
Arguments:
- grad_fourier: bfloat16 [4, 1024, 2, 384], P('ma', 'lat'), may hold values from -6 to 6
- legendre: bfloat16 [4, 1024, 640], P('ma', 'lat'), may hold values from -0.1875 to 0.1875
- spectra: bfloat16 [640, 4, 2, 384], P('lat', None, None, 'ma'), may hold values from -3 to 3
- filter_weight: float32 [640, 2, 384], P('lat'), may hold values from -6 to 6
Outputs:
- input_grad: float32 [640, 4, 2, 384], P('lat', 'ma')
- weight_grad: float32 [640, 2, 384], P('lat', None, 'ma')
All inputs are finite; a program needn't handle non-finite values.
Results may differ from a plain program's by a relative error of at most 0.0006.
Values may be sent and summed in bfloat16 or wider, within the bound.
A program may use at most 64 MiB of HBM per device.

v0:
```python
import functools

import jax
import jax.numpy as jnp
from jax import lax
from jax.experimental import pallas as pl
from jax.experimental.pallas import tpu as pltpu
from jax.sharding import PartitionSpec as P

MESH = pl.DeviceIdType.MESH
GROUP = 8
CORE, NEAR, FAR = 1, 2, 4


def kernel(sizes, leg_hbm, rows_ref, spec_ref, grads_ref, wgrad_ref, leg_ref, tab_send, tab_all, lhs, rows_out, rows_all,
           part, part_recv, value_all, spec_all, wpart, wrecv, leg_sem, tab_ssem, tab_rsem, row_ssem, row_rsem, part_ssem,
           part_rsem, spec_ssem, spec_rsem, w_ssem, w_rsem):
    n, ma, orders, rows, deg, dq, chans, cuts = sizes
    blocks = n // GROUP
    chunks = ma * cuts
    width = chans // ma
    lanes = 2 * width // cuts
    lat = lax.axis_index("lat")
    mine = lax.axis_index("ma")
    spot = lax.rem(lat, GROUP)
    block = lax.div(lat, GROUP)
    bits = [lax.rem(lax.div(spot, 1 << b), 2) for b in range(3)]
    own = [bits[0], 1 - bits[0]]

    def member(slot):
        at = 0
        for b in range(3):
            bit = 1 - bits[b] if slot >> b & 1 else bits[b]
            at = at + bit * (1 << b)
        return at

    def peer(slot, step=0):
        return (other_block(step) * GROUP + member(slot), mine)

    def other_block(step):
        return lax.rem(block + step, blocks)

    def other_ma(step):
        return lax.rem(mine + step, ma)

    barrier = pltpu.get_barrier_semaphore()
    partners = [peer(slot) for slot in range(1, GROUP)]
    partners += [peer(slot, step) for step in range(1, blocks) for slot in (0, CORE)]
    partners += [(lat, other_ma(step)) for step in range(1, ma)]
    for device in partners:
        pl.semaphore_signal(barrier, inc=1, device_id=device, device_id_type=MESH)
    leg_copy = pltpu.make_async_copy(leg_hbm, leg_ref, leg_sem)
    leg_copy.start()

    for q in range(ma):
        place = lax.rem(q - mine - 1 + 2 * ma, ma)
        cut = slice(q * width, (q + 1) * width)
        for e in range(2):
            both = jnp.concatenate([rows_ref[2 * own[e]][:, cut], rows_ref[2 * own[e] + 1][:, cut]], axis=1)
            for part_at in range(cuts):
                piece = both[:, part_at * lanes:(part_at + 1) * lanes]
                if e == 0:
                    rows_all[place * cuts + part_at, 0] = piece
                else:
                    rows_out[place * cuts + part_at] = piece
    pl.semaphore_wait(barrier, len(partners))

    def copy(src, dst, ssem, rsem, device):
        return pltpu.make_async_remote_copy(
            src_ref=src, dst_ref=dst, send_sem=ssem, recv_sem=rsem, device_id=device, device_id_type=MESH)

    row_copies = {}

    def send_rows(k, src, slot, via):
        row_copies[k, slot] = copy(src, rows_all.at[k, slot], row_ssem.at[k, slot], row_rsem.at[k, slot], peer(via))
        row_copies[k, slot].start()

    def first(k):
        for via in (FAR, FAR + CORE, NEAR, NEAR + CORE, CORE):
            send_rows(k, rows_out.at[k] if via & CORE else rows_all.at[k, 0], via, via)

    first(0)

    leg_copy.wait()
    total = leg_ref.shape[2]
    degree = lax.broadcasted_iota(jnp.int32, (orders, rows, total), 2)
    order = lax.broadcasted_iota(jnp.int32, (orders, rows, total), 0) + mine * orders
    table = jnp.where(degree >= order, leg_ref[...].astype(jnp.float32), 0.0)
    turned = table.reshape(orders * rows, total).T
    half = blocks // 2
    for pair in range(GROUP // 2):
        halves = []
        for f in range(2):
            parts = []
            for b in range(f * half, (f + 1) * half):
                for c in range(2):
                    start = (b * GROUP + pair * 2 + c) * deg
                    parts.append(turned[start:start + deg])
                    if dq > deg:
                        parts.append(jnp.zeros((dq - deg, orders * rows), jnp.float32))
            halves.append(jnp.concatenate(parts, axis=0))
        for m in range(orders):
            tab_send[pair * 2 + m] = jnp.concatenate(
                [each[:, m * rows:(m + 1) * rows] for each in halves], axis=1).astype(jnp.bfloat16)

    tab_copies = {}
    for slot in (FAR, NEAR, FAR + NEAR, FAR + CORE, NEAR + CORE, FAR + NEAR + CORE, CORE):
        tab_copies[slot] = copy(tab_send.at[member(slot)], tab_all.at[slot], tab_ssem.at[slot], tab_rsem.at[slot], peer(slot))
        tab_copies[slot].start()
    first(1)
    spec_copies = []
    for step in range(1, ma):
        to = other_ma(step)
        spec_copies.append(copy(spec_ref.at[to], spec_all.at[mine], spec_ssem.at[step], spec_rsem.at[step], (lat, to)))
        spec_copies[-1].start()
    spec_all[mine] = spec_ref[mine]

    def spread(k):
        for slot in (FAR, FAR + CORE):
            row_copies[k, slot].wait_recv()
            send_rows(k, rows_all.at[k, slot], slot + NEAR, NEAR)
        if k + 2 < chunks:
            first(k + 2)

    part_copies = {}

    def multiply(k):
        if k == 0:
            for slot in tab_copies:
                tab_copies[slot].wait_recv()
            tabs = [tab_send[spot]] + [tab_all[slot] for slot in range(1, GROUP)]
            tabs = [t.astype(jnp.float32) for t in tabs]
            lhs[...] = jnp.concatenate(
                [jnp.concatenate([t[:, f * rows:(f + 1) * rows] for t in tabs], axis=1) for f in range(2)], axis=0
            ).astype(jnp.bfloat16)
        for slot in (CORE, NEAR, NEAR + CORE, FAR + NEAR, FAR + NEAR + CORE):
            row_copies[k, slot].wait_recv()
        product = jnp.dot(lhs[...], rows_all[k].reshape(GROUP * rows, lanes), preferred_element_type=jnp.float32)
        part[k] = product.reshape(2 * blocks, dq, lanes)
        for step in range(1, blocks + 1):
            step = step % blocks
            for e in range(2):
                if step or e:
                    part_copies[k, step, e] = copy(
                        part.at[k, other_block(step) * 2 + own[e]], part_recv.at[k, step, e], part_ssem.at[k, step, e],
                        part_rsem.at[k, step, e], peer(e * CORE, step))
                    part_copies[k, step, e].start()

    w_copies = []

    def finish(turn):
        step = (turn + 1) % ma
        q = other_ma(step)
        if turn == 0:
            for each in spec_copies:
                each.wait_recv()
        real, imag = 0.0, 0.0
        for e in range(2):
            pieces = []
            for k in range(turn * cuts, (turn + 1) * cuts):
                piece = part[k, block * 2 + own[0]] if e == 0 else None
                for s in range(0 if e else 1, blocks):
                    part_copies[k, s, e].wait_recv()
                    piece = part_recv[k, s, e] if piece is None else piece + part_recv[k, s, e]
                pieces.append(piece)
            value = jnp.concatenate(pieces, axis=1)
            value_all[q * orders + own[e]] = value
            real_grad = value[:, :width]
            imag_grad = value[:, width:]
            stored = spec_all[q, own[e]].astype(jnp.float32)
            real_store = stored[:dq]
            imag_store = stored[dq:]
            real = real + real_store * real_grad + imag_store * imag_grad
            imag = imag + real_store * imag_grad - imag_store * real_grad
        wpart[step, 0] = real
        wpart[step, 1] = imag
        if step > 0:
            w_copies.append(copy(wpart.at[step], wrecv.at[step], w_ssem.at[step], w_rsem.at[step], (lat, q)))
            w_copies[-1].start()

    spread(0)
    for k in range(chunks):
        if k + 1 < chunks:
            spread(k + 1)
        multiply(k)
    for turn in range(ma):
        finish(turn)

    for m in range(orders):
        for r in range(2):
            grads_ref[m, r] = jnp.concatenate(
                [value_all[q * orders + m][:, r * width:(r + 1) * width] for q in range(ma)], axis=1)
    weight = wpart[0]
    for step in range(1, ma):
        w_copies[step - 1].wait_recv()
        weight = weight + wrecv[step]
    wgrad_ref[...] = weight

    for each in [*tab_copies.values(), *row_copies.values(), *part_copies.values(), *spec_copies, *w_copies]:
        each.wait_send()


def body(n, ma, grad_fourier, legendre, spectra, filter_weight):
    orders, rows, _, chans = grad_fourier.shape
    deg = filter_weight.shape[0]
    dq = -(-deg // 8) * 8
    width = chans // ma
    cuts = max(2 * width // 128, 1)
    chunks = ma * cuts
    lanes = 2 * width // cuts
    blocks = n // GROUP
    flat_rows = grad_fourier.transpose(0, 2, 1, 3).reshape(2 * orders, rows, chans)
    spec = jnp.pad(spectra, ((0, dq - deg), (0, 0), (0, 0), (0, 0))).transpose(1, 2, 0, 3)
    spec = spec.reshape(ma, orders, 2 * dq, width)
    vmem = pl.BlockSpec(memory_space=pltpu.VMEM)
    dma = pltpu.SemaphoreType.DMA
    grads, wgrad = pl.pallas_call(
        functools.partial(kernel, (n, ma, orders, rows, deg, dq, chans, cuts)),
        out_shape=(
            jax.ShapeDtypeStruct((orders, 2, dq, chans), jnp.float32),
            jax.ShapeDtypeStruct((2, dq, width), jnp.float32),
        ),
        in_specs=[pl.BlockSpec(memory_space=pltpu.HBM), vmem, vmem],
        out_specs=(vmem, vmem),
        scratch_shapes=[
            pltpu.VMEM(legendre.shape, jnp.bfloat16),
            pltpu.VMEM((GROUP, blocks * dq, 2 * rows), jnp.bfloat16),
            pltpu.VMEM((GROUP, blocks * dq, 2 * rows), jnp.bfloat16),
            pltpu.VMEM((2 * blocks * dq, GROUP * rows), jnp.bfloat16),
            pltpu.VMEM((chunks, rows, lanes), jnp.bfloat16),
            pltpu.VMEM((chunks, GROUP, rows, lanes), jnp.bfloat16),
            pltpu.VMEM((chunks, 2 * blocks, dq, lanes), jnp.float32),
            pltpu.VMEM((chunks, blocks, 2, dq, lanes), jnp.float32),
            pltpu.VMEM((ma * orders, dq, 2 * width), jnp.float32),
            pltpu.VMEM((ma, orders, 2 * dq, width), jnp.bfloat16),
            pltpu.VMEM((ma, 2, dq, width), jnp.float32),
            pltpu.VMEM((ma, 2, dq, width), jnp.float32),
            dma(()),
            dma((GROUP,)), dma((GROUP,)),
            dma((chunks, GROUP)), dma((chunks, GROUP)),
            dma((chunks, blocks, 2)), dma((chunks, blocks, 2)),
            dma((ma,)), dma((ma,)),
            dma((ma,)), dma((ma,)),
        ],
        compiler_params=pltpu.CompilerParams(
            collective_id=0, has_side_effects=True, vmem_limit_bytes=24 * 1024 * 1024),
        cost_estimate=pl.CostEstimate(
            flops=4 * orders * blocks * dq * GROUP * rows * chans, bytes_accessed=8 * orders * dq * chans, transcendentals=0),
    )(legendre, flat_rows, spec)
    grads = grads[:, :, :deg].transpose(2, 0, 1, 3)
    real_grad = grads[:, :, 0, :]
    imag_grad = grads[:, :, 1, :]
    real_weight = filter_weight[:, None, 0, :]
    imag_weight = filter_weight[:, None, 1, :]
    input_grad = jnp.stack(
        [
            real_weight * real_grad + imag_weight * imag_grad,
            real_weight * imag_grad - imag_weight * real_grad,
        ],
        axis=2,
    )
    return input_grad, wgrad[:, :deg].transpose(1, 0, 2)


def solution(mesh):
    in_specs = (
        P("ma", "lat", None, None),
        P("ma", "lat", None),
        P("lat", None, None, "ma"),
        P("lat", None, None),
    )
    out_specs = (P("lat", "ma", None, None), P("lat", None, "ma"))
    fn = functools.partial(body, mesh.shape["lat"], mesh.shape["ma"])
    return jax.shard_map(fn, mesh=mesh, in_specs=in_specs, out_specs=out_specs, check_vma=False)
```

profile of v0, /device:TPU:0, one launch (start us, length us, event | category | flops | bytes accessed | tf_op | source)
XLA Modules:
  0.0 30.1 jit_solution(17283692801420247652)
XLA Ops:
  0.6 0.0 copy-start.1
  0.6 1.0 %copy.11 = bf16[2,2,64,384]{3,2,1,0:T(8,128)(2,1)S(1)} copy(bf16[2,2,64,384]{3,1,2,0:T(2,128)(2,1)} %bitcast.14) | data formatting | bytes 393216 | tf_op jit(solution)/shard_map/transpose | solution.py:212
  1.6 0.0 copy-done.1
  1.6 0.0 copy-start
  1.7 0.9 %copy-done = bf16[2,64,640]{2,1,0:T(8,128)(2,1)S(1)} copy-done((bf16[2,64,640]{2,1,0:T(8,128)(2,1)S(1)}, bf16[2,64,640]{2,1,0:T(8,128)(2,1)}, u32[]{:S(2)}) %copy-start) | copy-done | bytes 163864
  2.6 0.0 copy-start.2
  2.6 25.8 %shard_map.59 = (f32[2,2,40,384]{3,2,1,0:T(8,128)S(1)}, f32[2,40,192]{2,1,0:T(8,128)S(1)}) custom-call(bf16[2,64,640]{2,1,0:T(8,128)(2,1)S(1)} %copy-done, bf16[4,64,384]{2,1,0:T(8,128)(2,1)S(1)} %bitcast.10, bf16[2,2,80,192]{3,2,1,0:T(8,128)(2,1)S(1)} %bitcast.11), custom_call_target="tpu_custom_call" | custom-call | flops 125829120 | bytes 245760 | tf_op jit(solution)/shard_map/pallas_call | solution.py:217
  28.4 0.0 copy-done.2
  28.4 0.1 fusion
  28.6 0.8 %copy.14 = f32[40,2,2,384]{3,2,1,0:T(2,128)} copy(f32[40,2,2,384]{3,0,2,1:T(8,128)S(1)} %pad_maximum_fusion) | data formatting | bytes 491520
  29.4 0.7 %copy.15 = f32[40,2,192]{2,1,0:T(2,128)} copy(f32[40,2,192]{2,0,1:T(8,128)S(1)} %bitcast.13) | data formatting | bytes 122880
  (4 shorter events, 0.1 us)
Async XLA Ops:
  0.6 1.0 %copy-start.1 = (bf16[40,4,2,192]{3,2,1,0:T(2,128)(2,1)S(1)}, bf16[40,4,2,192]{3,2,1,0:T(2,128)(2,1)}, u32[]{:S(2)}) copy-start(bf16[40,4,2,192]{3,2,1,0:T(2,128)(2,1)} %param.6) | copy-start | bytes 368644
  1.6 0.9 %copy-start = (bf16[2,64,640]{2,1,0:T(8,128)(2,1)S(1)}, bf16[2,64,640]{2,1,0:T(8,128)(2,1)}, u32[]{:S(2)}) copy-start(bf16[2,64,640]{2,1,0:T(8,128)(2,1)} %leg_hbm.1) | copy-start | bytes 491524
  2.6 25.8 %copy-start.2 = (f32[40,2,384]{2,1,0:T(2,128)S(1)}, f32[40,2,384]{2,1,0:T(2,128)}, u32[]{:S(2)}) copy-start(f32[40,2,384]{2,1,0:T(2,128)} %param.7) | copy-start | bytes 368644
where the time goes:
time: 30.3 us; the launch traced here: 30.1 us
  Pallas kernels  25.8 us (85%)
  local copies, waits for them, and re-layouts  3.51 us (12%)
  between operations  0.7 us (2%)
    pallas_call x1, Pallas kernels, body(): pl.pallas_call(functools.partial(kernel, (n, ma, orders, rows, deg, dq, c...  25.8 us
    unnamed x8, local copies, waits for them, and re-layouts  2.39 us
    transpose x1, local copies, waits for them, and re-layouts, body(): grad_fourier.transpose(0, 2, 1, 3).reshape(2 * orders, rows, chans)  0.99 us

commit v1 on v0

--- a/solution.py
+++ b/solution.py
@@ -12,8 +12,8 @@
 CORE, NEAR, FAR = 1, 2, 4
 
 
-def kernel(sizes, leg_hbm, rows_ref, spec_ref, grads_ref, wgrad_ref, leg_ref, tab_send, tab_all, lhs, rows_out, rows_all,
-           part, part_recv, value_all, spec_all, wpart, wrecv, leg_sem, tab_ssem, tab_rsem, row_ssem, row_rsem, part_ssem,
+def kernel(sizes, leg_ref, rows_ref, spec_ref, grads_ref, wgrad_ref, tab_send, tab_all, lhs, rows_out, rows_all,
+           part, part_recv, value_all, spec_all, wpart, wrecv, tab_ssem, tab_rsem, row_ssem, row_rsem, part_ssem,
            part_rsem, spec_ssem, spec_rsem, w_ssem, w_rsem):
     n, ma, orders, rows, deg, dq, chans, cuts = sizes
     blocks = n // GROUP
@@ -49,8 +49,6 @@
     partners += [(lat, other_ma(step)) for step in range(1, ma)]
     for device in partners:
         pl.semaphore_signal(barrier, inc=1, device_id=device, device_id_type=MESH)
-    leg_copy = pltpu.make_async_copy(leg_hbm, leg_ref, leg_sem)
-    leg_copy.start()
 
     for q in range(ma):
         place = lax.rem(q - mine - 1 + 2 * ma, ma)
@@ -81,12 +79,7 @@
 
     first(0)
 
-    leg_copy.wait()
-    total = leg_ref.shape[2]
-    degree = lax.broadcasted_iota(jnp.int32, (orders, rows, total), 2)
-    order = lax.broadcasted_iota(jnp.int32, (orders, rows, total), 0) + mine * orders
-    table = jnp.where(degree >= order, leg_ref[...].astype(jnp.float32), 0.0)
-    turned = table.reshape(orders * rows, total).T
+    turned = leg_ref[...].astype(jnp.float32).reshape(orders * rows, leg_ref.shape[2]).T
     half = blocks // 2
     for pair in range(GROUP // 2):
         halves = []
@@ -183,8 +176,9 @@
         if k + 1 < chunks:
             spread(k + 1)
         multiply(k)
-    for turn in range(ma):
-        finish(turn)
+        if k % cuts == max(cuts - 2, 0) and k >= cuts:
+            finish(k // cuts - 1)
+    finish(ma - 1)
 
     for m in range(orders):
         for r in range(2):
@@ -210,6 +204,9 @@
     lanes = 2 * width // cuts
     blocks = n // GROUP
     flat_rows = grad_fourier.transpose(0, 2, 1, 3).reshape(2 * orders, rows, chans)
+    degree = lax.broadcasted_iota(jnp.int32, legendre.shape, 2)
+    order = lax.broadcasted_iota(jnp.int32, legendre.shape, 0) + lax.axis_index("ma") * orders
+    table = jnp.where(degree >= order, legendre, jnp.zeros_like(legendre))
     spec = jnp.pad(spectra, ((0, dq - deg), (0, 0), (0, 0), (0, 0))).transpose(1, 2, 0, 3)
     spec = spec.reshape(ma, orders, 2 * dq, width)
     vmem = pl.BlockSpec(memory_space=pltpu.VMEM)
@@ -220,10 +217,9 @@
             jax.ShapeDtypeStruct((orders, 2, dq, chans), jnp.float32),
             jax.ShapeDtypeStruct((2, dq, width), jnp.float32),
         ),
-        in_specs=[pl.BlockSpec(memory_space=pltpu.HBM), vmem, vmem],
+        in_specs=[vmem] * 3,
         out_specs=(vmem, vmem),
         scratch_shapes=[
-            pltpu.VMEM(legendre.shape, jnp.bfloat16),
             pltpu.VMEM((GROUP, blocks * dq, 2 * rows), jnp.bfloat16),
             pltpu.VMEM((GROUP, blocks * dq, 2 * rows), jnp.bfloat16),
             pltpu.VMEM((2 * blocks * dq, GROUP * rows), jnp.bfloat16),
@@ -235,7 +231,6 @@
             pltpu.VMEM((ma, orders, 2 * dq, width), jnp.bfloat16),
             pltpu.VMEM((ma, 2, dq, width), jnp.float32),
             pltpu.VMEM((ma, 2, dq, width), jnp.float32),
-            dma(()),
             dma((GROUP,)), dma((GROUP,)),
             dma((chunks, GROUP)), dma((chunks, GROUP)),
             dma((chunks, blocks, 2)), dma((chunks, blocks, 2)),
@@ -246,7 +241,7 @@
             collective_id=0, has_side_effects=True, vmem_limit_bytes=24 * 1024 * 1024),
         cost_estimate=pl.CostEstimate(
             flops=4 * orders * blocks * dq * GROUP * rows * chans, bytes_accessed=8 * orders * dq * chans, transcendentals=0),
-    )(legendre, flat_rows, spec)
+    )(table, flat_rows, spec)
     grads = grads[:, :, :deg].transpose(2, 0, 1, 3)
     real_grad = grads[:, :, 0, :]
     imag_grad = grads[:, :, 1, :]

time: 30.3 us -> 30.5 us (level)
  other arithmetic: 0.05 us -> 1.11 us
  local copies, waits for them, and re-layouts: 3.51 us -> 2.55 us
    select_n x0 -> x1, other arithmetic: none -> 1.05 us  [body(): table = jnp.where(degree >= order, legendre, jnp.zeros_like(legendre))]
    transpose x1, local copies, waits for them, and re-layouts: 0.99 us -> 0.03 us  [body(): grad_fourier.transpose(0, 2, 1, 3).reshape(2 * orders, rows, chans)]
where the time goes in v1:
time: 30.5 us; the launch traced here: 30.3 us
  Pallas kernels  25.9 us (85%)
  local copies, waits for them, and re-layouts  2.55 us (8%)
  other arithmetic  1.11 us (4%)
  between operations  0.73 us (2%)
    pallas_call x1, Pallas kernels, body(): pl.pallas_call(functools.partial(kernel, (n, ma, orders, rows, deg, dq, c...  25.9 us
    unnamed x8, local copies, waits for them, and re-layouts  2.39 us
    select_n x1, other arithmetic, body(): table = jnp.where(degree >= order, legendre, jnp.zeros_like(legendre))  1.05 us

profile of v1, /device:TPU:0, one launch (start us, length us, event | category | flops | bytes accessed | tf_op | source)
XLA Modules:
  0.0 30.3 jit_solution(10725024302422193309)
XLA Ops:
  0.6 0.0 copy-start
  0.7 1.1 %fusion.leg_ref = bf16[2,64,640]{2,1,0:T(8,128)(2,1)S(1)} fusion(bf16[2,64,640]{2,1,0:T(8,128)(2,1)} %param.5, s32[2]{0:T(128)S(1)} %iota_add_fusion), kind=kLoop, calls=%fused_computation.1 | loop fusion | flops 163840 | bytes 327688 | tf_op jit(solution)/shard_map/jit(_where)/select_n | solution.py:209
  1.7 0.0 copy-done
  1.7 0.0 copy-start.1
  1.8 0.9 %copy-done.1 = bf16[40,4,2,192]{3,2,1,0:T(2,128)(2,1)S(1)} copy-done((bf16[40,4,2,192]{3,2,1,0:T(2,128)(2,1)S(1)}, bf16[40,4,2,192]{3,2,1,0:T(2,128)(2,1)}, u32[]{:S(2)}) %copy-start.1) | copy-done | bytes 122904
  2.7 0.0 copy-start.2
  2.7 25.9 %shard_map.59 = (f32[2,2,40,384]{3,2,1,0:T(8,128)S(1)}, f32[2,40,192]{2,1,0:T(8,128)S(1)}) custom-call(bf16[2,64,640]{2,1,0:T(8,128)(2,1)S(1)} %fusion.leg_ref, bf16[4,64,384]{2,1,0:T(8,128)(2,1)S(1)} %bitcast.10, bf16[2,2,80,192]{3,2,1,0:T(8,128)(2,1)S(1)} %bitcast.11), custom_call_target="tpu_custom_call" | custom-call | flops 125829120 | bytes 245760 | tf_op jit(solution)/shard_map/pallas_call | solution.py:214
  28.6 0.0 copy-done.2
  28.6 0.1 fusion.1
  28.8 0.8 %copy.14 = f32[40,2,2,384]{3,2,1,0:T(2,128)} copy(f32[40,2,2,384]{3,0,2,1:T(8,128)S(1)} %pad_maximum_fusion) | data formatting | bytes 491520
  29.6 0.7 %copy.15 = f32[40,2,192]{2,1,0:T(2,128)} copy(f32[40,2,192]{2,0,1:T(8,128)S(1)} %bitcast.13) | data formatting | bytes 122880
  (6 shorter events, 0.1 us)
Async XLA Ops:
  0.6 1.1 %copy-start = (bf16[2,64,2,384]{3,2,1,0:T(2,128)(2,1)S(1)}, bf16[2,64,2,384]{3,2,1,0:T(2,128)(2,1)}, u32[]{:S(2)}) copy-start(bf16[2,64,2,384]{3,2,1,0:T(2,128)(2,1)} %param.4) | copy-start | bytes 589828
  1.7 0.9 %copy-start.1 = (bf16[40,4,2,192]{3,2,1,0:T(2,128)(2,1)S(1)}, bf16[40,4,2,192]{3,2,1,0:T(2,128)(2,1)}, u32[]{:S(2)}) copy-start(bf16[40,4,2,192]{3,2,1,0:T(2,128)(2,1)} %param.6) | copy-start | bytes 368644
  2.7 25.9 %copy-start.2 = (f32[40,2,384]{2,1,0:T(2,128)S(1)}, f32[40,2,384]{2,1,0:T(2,128)}, u32[]{:S(2)}) copy-start(f32[40,2,384]{2,1,0:T(2,128)} %param.7) | copy-start | bytes 368644

commit v2 on v0

--- a/solution.py
+++ b/solution.py
@@ -20,6 +20,7 @@
     chunks = ma * cuts
     width = chans // ma
     lanes = 2 * width // cuts
+    ahead = min(3, chunks)
     lat = lax.axis_index("lat")
     mine = lax.axis_index("ma")
     spot = lax.rem(lat, GROUP)
@@ -107,7 +108,8 @@
     for slot in (FAR, NEAR, FAR + NEAR, FAR + CORE, NEAR + CORE, FAR + NEAR + CORE, CORE):
         tab_copies[slot] = copy(tab_send.at[member(slot)], tab_all.at[slot], tab_ssem.at[slot], tab_rsem.at[slot], peer(slot))
         tab_copies[slot].start()
-    first(1)
+    for k in range(1, ahead):
+        first(k)
     spec_copies = []
     for step in range(1, ma):
         to = other_ma(step)
@@ -119,8 +121,8 @@
         for slot in (FAR, FAR + CORE):
             row_copies[k, slot].wait_recv()
             send_rows(k, rows_all.at[k, slot], slot + NEAR, NEAR)
-        if k + 2 < chunks:
-            first(k + 2)
+        if k + ahead < chunks:
+            first(k + ahead)
 
     part_copies = {}
 
@@ -183,8 +185,9 @@
         if k + 1 < chunks:
             spread(k + 1)
         multiply(k)
-    for turn in range(ma):
-        finish(turn)
+        if k % cuts == max(cuts - 2, 0) and k >= cuts:
+            finish(k // cuts - 1)
+    finish(ma - 1)
 
     for m in range(orders):
         for r in range(2):

time: 30.3 us -> 31.2 us (1.030)
  Pallas kernels: 25.8 us -> 26.7 us
    pallas_call x1, Pallas kernels: 25.8 us -> 26.7 us  [body(): pl.pallas_call(functools.partial(kernel, (n, ma, orders, rows, deg, dq, c...]
where the time goes in v2:
time: 31.2 us; the launch traced here: 31 us
  Pallas kernels  26.7 us (86%)
  local copies, waits for them, and re-layouts  3.51 us (11%)
  between operations  0.7 us (2%)
    pallas_call x1, Pallas kernels, body(): pl.pallas_call(functools.partial(kernel, (n, ma, orders, rows, deg, dq, c...  26.7 us
    unnamed x8, local copies, waits for them, and re-layouts  2.39 us
    transpose x1, local copies, waits for them, and re-layouts, body(): grad_fourier.transpose(0, 2, 1, 3).reshape(2 * orders, rows, chans)  0.99 us

profile of v2, /device:TPU:0, one launch (start us, length us, event | category | flops | bytes accessed | tf_op | source)
XLA Modules:
  0.0 31.0 jit_solution(1050851088119523888)
XLA Ops:
  0.6 0.0 copy-start.1
  0.6 1.0 %copy.11 = bf16[2,2,64,384]{3,2,1,0:T(8,128)(2,1)S(1)} copy(bf16[2,2,64,384]{3,1,2,0:T(2,128)(2,1)} %bitcast.14) | data formatting | bytes 393216 | tf_op jit(solution)/shard_map/transpose | solution.py:215
  1.6 0.0 copy-done.1
  1.6 0.0 copy-start
  1.7 0.9 %copy-done = bf16[2,64,640]{2,1,0:T(8,128)(2,1)S(1)} copy-done((bf16[2,64,640]{2,1,0:T(8,128)(2,1)S(1)}, bf16[2,64,640]{2,1,0:T(8,128)(2,1)}, u32[]{:S(2)}) %copy-start) | copy-done | bytes 163864
  2.6 0.0 copy-start.2
  2.6 26.7 %shard_map.59 = (f32[2,2,40,384]{3,2,1,0:T(8,128)S(1)}, f32[2,40,192]{2,1,0:T(8,128)S(1)}) custom-call(bf16[2,64,640]{2,1,0:T(8,128)(2,1)S(1)} %copy-done, bf16[4,64,384]{2,1,0:T(8,128)(2,1)S(1)} %bitcast.10, bf16[2,2,80,192]{3,2,1,0:T(8,128)(2,1)S(1)} %bitcast.11), custom_call_target="tpu_custom_call" | custom-call | flops 125829120 | bytes 245760 | tf_op jit(solution)/shard_map/pallas_call | solution.py:220
  29.3 0.0 copy-done.2
  29.3 0.1 fusion
  29.5 0.8 %copy.14 = f32[40,2,2,384]{3,2,1,0:T(2,128)} copy(f32[40,2,2,384]{3,0,2,1:T(8,128)S(1)} %pad_maximum_fusion) | data formatting | bytes 491520
  30.3 0.7 %copy.15 = f32[40,2,192]{2,1,0:T(2,128)} copy(f32[40,2,192]{2,0,1:T(8,128)S(1)} %bitcast.13) | data formatting | bytes 122880
  (4 shorter events, 0.1 us)
Async XLA Ops:
  0.6 1.0 %copy-start.1 = (bf16[40,4,2,192]{3,2,1,0:T(2,128)(2,1)S(1)}, bf16[40,4,2,192]{3,2,1,0:T(2,128)(2,1)}, u32[]{:S(2)}) copy-start(bf16[40,4,2,192]{3,2,1,0:T(2,128)(2,1)} %param.6) | copy-start | bytes 368644
  1.6 0.9 %copy-start = (bf16[2,64,640]{2,1,0:T(8,128)(2,1)S(1)}, bf16[2,64,640]{2,1,0:T(8,128)(2,1)}, u32[]{:S(2)}) copy-start(bf16[2,64,640]{2,1,0:T(8,128)(2,1)} %leg_hbm.1) | copy-start | bytes 491524
  2.6 26.8 %copy-start.2 = (f32[40,2,384]{2,1,0:T(2,128)S(1)}, f32[40,2,384]{2,1,0:T(2,128)}, u32[]{:S(2)}) copy-start(f32[40,2,384]{2,1,0:T(2,128)} %param.7) | copy-start | bytes 368644
